TPU v7x, 32 devices: a whole 2x2x4 slice. The times are simulated.
32 devices in a mesh: seg: 4 (over z), sec: 8 (over y, x, core).
Axes of the slice: x: 2, y: 2, z: 4, core: 2. Of those that a mesh axis runs over, the one named last changes fastest.
Arguments:
- wave_block: bfloat16 [4, 2048, 64, 128], P('seg', 'sec'), may hold values from -6 to 6
- left_envs: bfloat16 [4, 64, 128, 24, 128], P('seg', 'sec'), may hold values from -0.109375 to 0.109375
- next_vectors: bfloat16 [4, 64, 128, 1024], P('seg', 'sec'), may hold values from -6 to 6
- site_weights: float32 [4, 24, 1024], P('seg'), may hold values from 0.5 to 2
- kept_counts: int32 [64], replicated, may hold values from 32 to 128
- slots_before: int32 [64], replicated, may hold values from 0 to 63, as said below
- slots_after: int32 [64], replicated, may hold values from 0 to 63, as said below
Outputs:
- mixed_out: bfloat16 [4, 64, 128, 1024], P('seg', 'sec')
Inputs may be any that keep to these rules, and one draw needn't show every extreme that they name: `slots_before`: A permutation of the sectors; device p of sec holds before-slots p * 8 to (p + 1) * 8 - 1. `slots_after`: A permutation of the sectors; device p of sec holds after-slots p * 8 to (p + 1) * 8 - 1. Of the sectors in one device's before-slots, at most 1 lie in any one device's after-slots, and exactly 1 for some pair of devices.
All inputs are finite; a program needn't handle non-finite values.
Results may differ from a plain program's by a relative error of at most 0.0058.
Values may be sent and summed in bfloat16 or wider, within the bound.
A program may use at most 192 MiB of HBM per device.

v0:
```python
import functools

import jax
import jax.numpy as jnp
from jax import lax
from jax.experimental import pallas as pl
from jax.experimental.pallas import tpu as pltpu
from jax.sharding import PartitionSpec as P

VMEM_BYTES = 48 * 1024 * 1024
PANEL = 8


def ring(value, axis, step):
    count = lax.axis_size(axis)
    return lax.ppermute(value, axis, [(i, (i + step) % count) for i in range(count)])


def inverse_of(slots):
    length_of = slots.shape[0]
    indices = jnp.arange(length_of, dtype=jnp.int32)
    return jnp.sum(jnp.where(slots[:, None] == indices[None, :], indices[:, None], 0), axis=0)


def pick(table, index):
    hits = index[:, None] == jnp.arange(table.shape[0], dtype=jnp.int32)[None, :]
    return jnp.sum(jnp.where(hits, table[None, :], 0), axis=1)


def place_for(owner, devices):
    hits = owner[None, :] == jnp.arange(devices, dtype=jnp.int32)[:, None]
    return jnp.sum(jnp.where(hits, jnp.arange(owner.shape[0], dtype=jnp.int32)[None, :], 0), axis=1)


def gram_kernel(place_ref, wave_ref, out_ref, wide):
    group = wave_ref.shape[1]
    rows = wave_ref.shape[0]
    wide[...] = wave_ref[...].astype(jnp.float32).reshape(wide.shape)
    base = pl.program_id(0) * group
    for s in range(group):
        x = wide[pl.ds(s, rows, stride=group), :].astype(jnp.bfloat16)
        out_ref[place_ref[base + s]] = lax.dot_general(
            x, x, (((0,), (0,)), ((), ())), preferred_element_type=jnp.float32
        )


def grams(wave, place):
    rows, sectors, block = wave.shape
    group = 16
    return pl.pallas_call(
        gram_kernel,
        grid_spec=pltpu.PrefetchScalarGridSpec(
            num_scalar_prefetch=1,
            grid=(sectors // group,),
            in_specs=[pl.BlockSpec((rows, group, block), lambda i, place: (0, i, 0))],
            out_specs=pl.BlockSpec((sectors, block, block), lambda i, place: (0, 0, 0)),
            scratch_shapes=[pltpu.VMEM((rows * group, block), jnp.float32)],
        ),
        out_shape=jax.ShapeDtypeStruct((sectors, block, block), jnp.float32),
        compiler_params=pltpu.CompilerParams(vmem_limit_bytes=VMEM_BYTES),
        cost_estimate=pl.CostEstimate(
            flops=2 * rows * sectors * block * block,
            bytes_accessed=2 * rows * sectors * block + 4 * sectors * block * block,
            transcendentals=0,
        ),
    )(place, wave)


def factor_kernel(total_rows, kept_ref, gram_ref, out_ref, c):
    width, size, _ = gram_ref.shape
    row_at = lax.broadcasted_iota(jnp.int32, (size, size), 0)
    col_at = lax.broadcasted_iota(jnp.int32, (size, size), 1)
    ridge = jnp.where(row_at == col_at, 0.1, 0.0).astype(jnp.float32)
    for s in range(width):
        c[pl.ds(s, size, stride=width), :] = gram_ref[s] * (1.0 / total_rows) + ridge
    lane = lax.broadcasted_iota(jnp.int32, (width, size), 1)

    def spread(row, at):
        return jnp.broadcast_to(row[:, at : at + 1], (width, size))

    for p in range(0, size, PANEL):
        rows = [c[(p + k) * width : (p + k + 1) * width, :] for k in range(PANEL)]
        corner = {
            (k, l): spread(rows[k], p + l) for k in range(PANEL) for l in range(k, PANEL)
        }
        inside = (lane >= p) & (lane < p + PANEL)
        rows = [
            jnp.where(inside, jnp.where(lane == p + k, 1.0, 0.0), rows[k]) for k in range(PANEL)
        ]
        for k in range(PANEL):
            pivot = corner[k, k]
            r = lax.rsqrt(pivot)
            r = r * (1.5 - 0.5 * pivot * r * r)
            rows[k] = rows[k] * r
            m = {l: corner[k, l] * r for l in range(k + 1, PANEL)}
            for l in range(k + 1, PANEL):
                for j in range(l, PANEL):
                    corner[l, j] = corner[l, j] - m[l] * m[j]
                rows[l] = rows[l] - m[l] * rows[k]
        for k in range(PANEL):
            c[(p + k) * width : (p + k + 1) * width, :] = rows[k]
        for i in range(p + PANEL, size):
            row = jnp.where(inside, 0.0, c[i * width : (i + 1) * width, :])
            first = spread(rows[0], i) * rows[0]
            second = spread(rows[1], i) * rows[1]
            for k in range(2, PANEL, 2):
                first += spread(rows[k], i) * rows[k]
                second += spread(rows[k + 1], i) * rows[k + 1]
            c[i * width : (i + 1) * width, :] = row - (first + second)
    for s in range(width):
        full = c[pl.ds(s, size, stride=width), :]
        keep = (col_at <= row_at) & (row_at < kept_ref[s])
        out_ref[s] = jnp.where(keep, full, 0.0).astype(out_ref.dtype)


def low_inverses(gram_sum, kept_here, total_rows):
    width, size, _ = gram_sum.shape
    return pl.pallas_call(
        functools.partial(factor_kernel, total_rows),
        in_specs=[
            pl.BlockSpec(memory_space=pltpu.SMEM),
            pl.BlockSpec(memory_space=pltpu.VMEM),
        ],
        out_specs=pl.BlockSpec(memory_space=pltpu.VMEM),
        out_shape=jax.ShapeDtypeStruct(gram_sum.shape, jnp.bfloat16),
        scratch_shapes=[pltpu.VMEM((size * width, size), jnp.float32)],
        compiler_params=pltpu.CompilerParams(vmem_limit_bytes=VMEM_BYTES),
        cost_estimate=pl.CostEstimate(
            flops=16 * size**3 * width, bytes_accessed=6 * size * size * width, transcendentals=0
        ),
    )(kept_here, gram_sum)


def matvec_kernel(
    channels, edge_ref, src_ref, dst_ref, low_ref, env_ref, vec_ref, weight_ref, out_ref, y, t
):
    low = low_ref[0]
    size = low.shape[0]
    columns = vec_ref.shape[2]

    @pl.when(edge_ref[0] == 0)
    def _():
        y[...] = lax.dot_general(
            env_ref[0], low, (((1,), (1,)), ((), ())), preferred_element_type=jnp.float32
        )

    @pl.when(edge_ref[0] != 0)
    def _():
        y[...] = jnp.zeros_like(y)
        y[pl.ds(0, size, stride=channels), :] = low.astype(jnp.float32).T

    for w in range(channels):
        part = y[pl.ds(w, size, stride=channels), :].astype(jnp.bfloat16)
        t[:, w * size : (w + 1) * size] = jnp.dot(
            low, part, preferred_element_type=jnp.float32
        ).astype(jnp.bfloat16)
    chunk = 256
    for at in range(0, columns, chunk):
        v = vec_ref[0, :, at : at + chunk].astype(jnp.float32)
        total = None
        for w in range(0, channels, 2):
            scaled = jnp.concatenate(
                [
                    (v * weight_ref[w + z : w + z + 1, at : at + chunk]).astype(jnp.bfloat16)
                    for z in range(2)
                ],
                axis=0,
            )
            term = jnp.dot(
                t[:, w * size : (w + 2) * size], scaled, preferred_element_type=jnp.float32
            )
            total = term if total is None else total + term
        out_ref[0, :, at : at + chunk] = total.astype(jnp.bfloat16)


def matvecs(low, env, vectors, weights, edge, src, dst, out_blocks):
    width, size, _ = low.shape
    channels = weights.shape[0]
    columns = weights.shape[1]
    return pl.pallas_call(
        functools.partial(matvec_kernel, channels),
        grid_spec=pltpu.PrefetchScalarGridSpec(
            num_scalar_prefetch=3,
            grid=(width,),
            in_specs=[
                pl.BlockSpec((1, size, size), lambda i, e, s, d: (i, 0, 0)),
                pl.BlockSpec((1, size * channels, size), lambda i, e, s, d: (i, 0, 0)),
                pl.BlockSpec((1, size, columns), lambda i, e, s, d: (s[i], 0, 0)),
                pl.BlockSpec((channels, columns), lambda i, e, s, d: (0, 0)),
            ],
            out_specs=pl.BlockSpec((1, size, columns), lambda i, e, s, d: (d[i], 0, 0)),
            scratch_shapes=[
                pltpu.VMEM((size * channels, size), jnp.float32),
                pltpu.VMEM((size, size * channels), jnp.bfloat16),
            ],
        ),
        out_shape=jax.ShapeDtypeStruct((out_blocks, size, columns), jnp.bfloat16),
        compiler_params=pltpu.CompilerParams(vmem_limit_bytes=VMEM_BYTES),
        cost_estimate=pl.CostEstimate(
            flops=2 * width * size * size * channels * (2 * size + columns),
            bytes_accessed=2 * width * size * (channels * size + 2 * columns),
            transcendentals=0,
        ),
    )(edge, src, dst, low, env, vectors, weights)


def copy_kernel(index_ref, in_ref, out_ref):
    out_ref[...] = in_ref[...]


def take_blocks(values, index):
    _, size, columns = values.shape
    return pl.pallas_call(
        copy_kernel,
        grid_spec=pltpu.PrefetchScalarGridSpec(
            num_scalar_prefetch=1,
            grid=(index.shape[0],),
            in_specs=[pl.BlockSpec((1, size, columns), lambda i, index: (index[i], 0, 0))],
            out_specs=pl.BlockSpec((1, size, columns), lambda i, index: (i, 0, 0)),
        ),
        out_shape=jax.ShapeDtypeStruct((index.shape[0], size, columns), values.dtype),
        cost_estimate=pl.CostEstimate(
            flops=0, bytes_accessed=4 * index.shape[0] * size * columns, transcendentals=0
        ),
    )(index, values)


def on_device(
    wave_block, left_envs, next_vectors, site_weights, kept_counts, slots_before, slots_after
):
    devices = lax.axis_size("sec")
    segments = lax.axis_size("seg")
    myself = lax.axis_index("sec")
    _, width, size, channels, _ = left_envs.shape
    total_rows = wave_block.shape[1] * devices
    inv_before = inverse_of(slots_before)
    inv_after = inverse_of(slots_after)
    mine_before = lax.dynamic_slice_in_dim(slots_before, myself * width, width)
    mine_after = lax.dynamic_slice_in_dim(slots_after, myself * width, width)
    before_owner = pick(inv_before, mine_after) // width
    after_owner = pick(inv_after, mine_before) // width

    gram_sum = lax.psum_scatter(
        grams(wave_block[0], inv_before), "sec", scatter_dimension=0, tiled=True
    )
    packed = take_blocks(next_vectors[0], place_for(before_owner, devices))
    arrived = lax.all_to_all(packed, "sec", split_axis=0, concat_axis=0, tiled=True)
    arrived = ring(arrived, "seg", -1)
    weights = ring(site_weights[0], "seg", -1)
    low = ring(low_inverses(gram_sum, pick(kept_counts, mine_before), total_rows), "seg", -1)
    edge = (lax.axis_index("seg") == segments - 1).astype(jnp.int32).reshape(1)
    env = left_envs[0].reshape(width, size * channels, size)
    result = matvecs(low, env, arrived, weights, edge, after_owner, after_owner, devices)
    result = ring(result, "seg", 1)
    returned = lax.all_to_all(result, "sec", split_axis=0, concat_axis=0, tiled=True)
    return take_blocks(returned, before_owner)[None]


def solution(mesh):
    placed = (
        P("seg", "sec", None, None),
        P("seg", "sec", None, None, None),
        P("seg", "sec", None, None),
        P("seg", None, None),
        P(),
        P(),
        P(),
    )
    return jax.shard_map(
        on_device,
        mesh=mesh,
        in_specs=placed,
        out_specs=P("seg", "sec", None, None),
        check_vma=False,
    )
```

profile of v0, /device:TPU:0, one launch (start us, length us, event | category | flops | bytes accessed | tf_op | source)
XLA Modules:
  0.0 229.7 jit_solution(5478117111284311688)
XLA Ops:
  6.5 0.0 reduce-scatter.2.cloned.1.call-start
  6.5 0.7 select_reduce_fusion.1.place_ref
  7.3 6.7 %shard_map.73 = f32[64,128,128]{2,1,0:T(8,128)S(1)} custom-call(s32[64]{0:T(128)S(1)} %select_reduce_fusion.1.place_ref, bf16[256,64,128]{2,1,0:T(8,128)(2,1)} %bitcast.6), custom_call_target="tpu_custom_call" | custom-call | flops 536870912 | bytes 8388608 | tf_op jit(solution)/shard_map/pallas_call | solution.py:50
  14.0 0.0 copy-start
  14.0 1.9 copy-done
  16.0 0.0 reduce-scatter.2.cloned.1.call-update
  16.0 0.6 copy-done.6
  16.6 0.1 dynamic_slice.6
  16.7 0.2 select_reduce_fusion.5
  16.9 0.6 select_reduce_fusion.2.index_ref
  17.5 6.3 %shard_map.75 = bf16[8,128,1024]{2,1,0:T(8,128)(2,1)} custom-call(s32[8]{0:T(128)} %select_reduce_fusion.2.index_ref, bf16[8,128,1024]{2,1,0:T(8,128)(2,1)} %bitcast.7), custom_call_target="tpu_custom_call" | custom-call | bytes 4194304 | tf_op jit(solution)/shard_map/pallas_call | solution.py:213
  23.8 0.0 copy-done.2
  23.9 0.0 copy-start.4
  23.9 43.3 %all_to_all.10 = bf16[8,128,1024]{2,1,0:T(8,128)(2,1)} all-to-all(bf16[8,128,1024]{2,1,0:T(8,128)(2,1)} %shard_map.75), channel_id=1, replica_groups=mesh['seg'=4,'sec'=8] {'sec'}, dimensions={0} | all-to-all | bytes 4194304 | tf_op jit(solution)/shard_map/all_to_all | solution.py:247
  67.2 4.2 %collective-permute-start.1 = (bf16[8,128,1024]{2,1,0:T(8,128)(2,1)}, bf16[8,128,1024]{2,1,0:T(8,128)(2,1)S(1)}, u32[]{:S(2)}, u32[]{:S(2)}) collective-permute-start(bf16[8,128,1024]{2,1,0:T(8,128)(2,1)} %all_to_all.10), channel_id=1, source_target_pairs={{0,24},{8,0},{16,8},{24,16},{1,25},{9,1},{17,9},{25,17},{2,26},{10... | collective-permute-start | bytes 6291464 | tf_op jit(solution)/shard_map/ppermute | solution.py:16
  71.4 0.0 copy-done.5
  71.4 0.1 dynamic_slice.7
  71.4 0.1 select_reduce_fusion
  71.5 0.2 select_reduce_fusion.3
  71.7 10.9 %reduce-scatter.2.cloned.1.call-done.gram_ref = f32[8,128,128]{2,1,0:T(8,128)} async-done(((f32[64,128,128]{2,1,0:T(8,128)}), f32[8,128,128]{2,1,0:T(8,128)}) %reduce-scatter.2.cloned.1.call-update) | async-done | bytes 524304 | tf_op jit(solution)/shard_map/reduce_scatter | solution.py:243
  82.7 1.0 copy-done.1
  83.7 16.4 %shard_map.74 = bf16[8,128,128]{2,1,0:T(8,128)(2,1)S(1)} custom-call(s32[8]{0:T(128)S(1)} %get-tuple-element.5.kept_ref, f32[8,128,128]{2,1,0:T(8,128)S(1)} %copy-done.1), custom_call_target="tpu_custom_call" | custom-call | flops 268435456 | bytes 786432 | tf_op jit(solution)/shard_map/pallas_call | solution.py:118
  100.2 3.4 %collective-permute-start = (bf16[8,128,128]{2,1,0:T(8,128)(2,1)S(1)}, bf16[8,128,128]{2,1,0:T(8,128)(2,1)S(1)}, u32[]{:S(2)}, u32[]{:S(2)}) collective-permute-start(bf16[8,128,128]{2,1,0:T(8,128)(2,1)S(1)} %shard_map.74), channel_id=1, source_target_pairs={{0,24},{8,0},{16,8},{24,16},{1,25},{9,1},{17,9},{25,17},{2,26},{10... | collective-permute-start | bytes 786440 | tf_op jit(solution)/shard_map/ppermute | solution.py:16
  103.6 0.5 collective-permute-start.2
  104.1 19.4 %collective-permute-done.2.weight_ref = f32[24,1024]{1,0:T(8,128)S(1)} collective-permute-done((f32[24,1024]{1,0:T(8,128)S(1)}, f32[24,1024]{1,0:T(8,128)S(1)}, u32[]{:S(2)}, u32[]{:S(2)}) %collective-permute-start.2) | collective-permute-done | bytes 98336 | tf_op jit(solution)/shard_map/ppermute | solution.py:16
  123.5 0.0 collective-permute-done.1.vec_ref
  123.5 0.0 collective-permute-done.low_ref
  123.5 15.6 %shard_map.76 = bf16[8,128,1024]{2,1,0:T(8,128)(2,1)S(1)} custom-call(s32[1]{0:T(128)} %bitcast.edge_ref, s32[8]{0:T(128)S(1)} %and_select_fusion.src_ref.dst_ref, s32[8]{0:T(128)S(1)} %and_select_fusion.src_ref.dst_ref, bf16[8,128,128]{2,1,0:T(8,128)(2,1)S(1)} %collective-permute-done.low_ref, bf16[8,3072,128]{2,1,0:T(8,128)(2,1)} %bitcast.8, ...), custom_call_target="tpu_custom_call" | custom-call | flops 8053063680 | bytes 10485760 | tf_op jit(solution)/shard_map/pallas_call | solution.py:180
  139.1 0.4 collective-permute-start.3
  139.6 47.2 %collective-permute-done.3 = bf16[8,128,1024]{2,1,0:T(8,128)(2,1)S(1)} collective-permute-done((bf16[8,128,1024]{2,1,0:T(8,128)(2,1)S(1)}, bf16[8,128,1024]{2,1,0:T(8,128)(2,1)S(1)}, u32[]{:S(2)}, u32[]{:S(2)}) %collective-permute-start.3) | collective-permute-done | bytes 2097184 | tf_op jit(solution)/shard_map/ppermute | solution.py:16
  186.8 29.7 %all_to_all.11.in_ref = bf16[8,128,1024]{2,1,0:T(8,128)(2,1)} all-to-all(bf16[8,128,1024]{2,1,0:T(8,128)(2,1)S(1)} %collective-permute-done.3), channel_id=1, replica_groups=mesh['seg'=4,'sec'=8] {'sec'}, dimensions={0} | all-to-all | bytes 4194304 | tf_op jit(solution)/shard_map/all_to_all | solution.py:255
  216.5 6.3 %shard_map.77 = bf16[8,128,1024]{2,1,0:T(8,128)(2,1)} custom-call(s32[8]{0:T(128)} %copy-done.2, bf16[8,128,1024]{2,1,0:T(8,128)(2,1)} %all_to_all.11.in_ref), custom_call_target="tpu_custom_call" | custom-call | bytes 4194304 | tf_op jit(solution)/shard_map/pallas_call | solution.py:213
  (9 shorter events, 0.0 us)
Async XLA Ops:
  6.5 76.1 %reduce-scatter.2.cloned.1.call-start = ((), (), s32[]{:S(2)}) async-start(), calls=%async_computation.3 | async-start | bytes 4718592 | tf_op jit(solution)/shard_map/reduce_scatter | solution.py:243
  14.0 1.9 copy-start
  16.0 0.7 copy-start.6
  16.9 7.0 %copy-start.2 = (s32[8]{0:T(128)}, s32[8]{0:T(128)S(1)}, u32[]{:S(2)}) copy-start(s32[8]{0:T(128)S(1)} %and_select_fusion.1.index_ref) | copy-start | bytes 100
  23.8 47.5 %copy-start.5 = (s32[64]{0:T(128)S(1)}, s32[64]{0:T(128)}, u32[]{:S(2)}) copy-start(s32[64]{0:T(128)} %param.12) | copy-start | bytes 772
  23.8 47.7 %copy-start.3 = (s32[64]{0:T(128)S(1)}, s32[64]{0:T(128)}, u32[]{:S(2)}) copy-start(s32[64]{0:T(128)} %param.11) | copy-start | bytes 772
  23.9 79.7 %copy-start.4 = (f32[1,24,1024]{2,1,0:T(8,128)S(1)}, f32[1,24,1024]{2,1,0:T(8,128)}, u32[]{:S(2)}) copy-start(f32[1,24,1024]{2,1,0:T(8,128)} %param.10) | copy-start | bytes 294916
  67.2 56.4 %collective-permute-start.1 = (bf16[8,128,1024]{2,1,0:T(8,128)(2,1)}, bf16[8,128,1024]{2,1,0:T(8,128)(2,1)S(1)}, u32[]{:S(2)}, u32[]{:S(2)}) collective-permute-start(bf16[8,128,1024]{2,1,0:T(8,128)(2,1)} %all_to_all.10), channel_id=1, source_target_pairs={{0,24},{8,0},{16,8},{24,16},{1,25},{9,1},{17,9},{25,17},{2,26},{10... | collective-permute-start | bytes 6291464 | tf_op jit(solution)/shard_map/ppermute | solution.py:16
  82.7 1.0 copy-start.1
  100.2 23.4 %collective-permute-start = (bf16[8,128,128]{2,1,0:T(8,128)(2,1)S(1)}, bf16[8,128,128]{2,1,0:T(8,128)(2,1)S(1)}, u32[]{:S(2)}, u32[]{:S(2)}) collective-permute-start(bf16[8,128,128]{2,1,0:T(8,128)(2,1)S(1)} %shard_map.74), channel_id=1, source_target_pairs={{0,24},{8,0},{16,8},{24,16},{1,25},{9,1},{17,9},{25,17},{2,26},{10... | collective-permute-start | bytes 786440 | tf_op jit(solution)/shard_map/ppermute | solution.py:16
  103.6 20.0 %collective-permute-start.2 = (f32[24,1024]{1,0:T(8,128)S(1)}, f32[24,1024]{1,0:T(8,128)S(1)}, u32[]{:S(2)}, u32[]{:S(2)}) collective-permute-start(f32[24,1024]{1,0:T(8,128)S(1)} %bitcast.9), channel_id=1, source_target_pairs={{0,24},{8,0},{16,8},{24,16},{1,25},{9,1},{17,9},{25,17},{2,26},{10... | collective-permute-start | bytes 294920 | tf_op jit(solution)/shard_map/ppermute | solution.py:16
  139.1 47.6 %collective-permute-start.3 = (bf16[8,128,1024]{2,1,0:T(8,128)(2,1)S(1)}, bf16[8,128,1024]{2,1,0:T(8,128)(2,1)S(1)}, u32[]{:S(2)}, u32[]{:S(2)}) collective-permute-start(bf16[8,128,1024]{2,1,0:T(8,128)(2,1)S(1)} %shard_map.76), channel_id=1, source_target_pairs={{0,8},{8,16},{16,24},{24,0},{1,9},{9,17},{17,25},{25,1},{2,10},{10... | collective-permute-start | bytes 6291464 | tf_op jit(solution)/shard_map/ppermute | solution.py:16
Sparse Core Ops, SparseCore 0:
  16.1 66.5 reduce-scatter.1
where the time goes:
time: 230 us
  waiting for transfers between devices  77.6 us (34%)
  blocking collectives  73 us (32%)
  Pallas kernels  51.4 us (22%)
  between operations  13.5 us (6%)
  starting transfers between devices  8.57 us (4%)
  local copies, waits for them, and re-layouts  3.75 us (2%)
    ppermute x4, waiting for transfers between devices, ring(): lax.ppermute(value, axis, [(i, (i + step) % count) for i in range(count)])  66.7 us
    all_to_all x1, blocking collectives, on_device(): lax.all_to_all(packed, 'sec', split_axis=0, concat_axis=0, tiled=True)  43.3 us
    all_to_all x1, blocking collectives, on_device(): lax.all_to_all(result, 'sec', split_axis=0, concat_axis=0, tiled=True)  29.7 us
    pallas_call x1, Pallas kernels, low_inverses(): pl.pallas_call(functools.partial(factor_kernel, total_rows), in_specs=[pl...  16.4 us
    pallas_call x1, Pallas kernels, matvecs(): pl.pallas_call(functools.partial(matvec_kernel, channels), grid_spec=pltp...  15.6 us
    pallas_call x2, Pallas kernels, take_blocks(): pl.pallas_call(copy_kernel, grid_spec=pltpu.PrefetchScalarGridSpec(num_sc...  12.6 us
    reduce_scatter x1, waiting for transfers between devices, on_device(): lax.psum_scatter(grams(wave_block[0], inv_before), 'sec', scatter_dimensi...  10.9 us
    ppermute x4, starting transfers between devices, ring(): lax.ppermute(value, axis, [(i, (i + step) % count) for i in range(count)])  8.57 us
  transfers between devices with their start and end apart: 5, of which 3 were waited for; matrix products, arithmetic and copies ran while one was open for 1% of the time, Pallas kernels for 10%

commit v1 on v0

v1 whole, which is shorter than its diff:
```python
import functools

import jax
import jax.numpy as jnp
from jax import lax
from jax.experimental import pallas as pl
from jax.experimental.pallas import tpu as pltpu
from jax.sharding import PartitionSpec as P

VMEM_BYTES = 48 * 1024 * 1024
PANEL = 8
MESH = pl.DeviceIdType.MESH


def ring(value, axis, step):
    count = lax.axis_size(axis)
    return lax.ppermute(value, axis, [(i, (i + step) % count) for i in range(count)])


def inverse_of(slots):
    length_of = slots.shape[0]
    indices = jnp.arange(length_of, dtype=jnp.int32)
    return jnp.sum(jnp.where(slots[:, None] == indices[None, :], indices[:, None], 0), axis=0)


def pick(table, index):
    hits = index[:, None] == jnp.arange(table.shape[0], dtype=jnp.int32)[None, :]
    return jnp.sum(jnp.where(hits, table[None, :], 0), axis=1)


def place_for(owner, order):
    hits = owner[None, :] == order[:, None]
    return jnp.sum(jnp.where(hits, jnp.arange(owner.shape[0], dtype=jnp.int32)[None, :], 0), axis=1)


def fold(full):
    size = full.shape[0]
    part, half = size // 4, size // 8
    lane = lax.broadcasted_iota(jnp.int32, (part, size), 1)
    second = jnp.where(
        lane < part, pltpu.roll(full[3 * part :], part, 1), full[part : 2 * part]
    )
    third = jnp.where(
        lane[:half] < 2 * part,
        pltpu.roll(full[2 * part + half : 3 * part], 2 * part, 1),
        full[2 * part : 2 * part + half],
    )
    return jnp.concatenate([full[:part], second, third], axis=0)


def unfold(packed, size):
    part, half = size // 4, size // 8
    second, third = packed[part : 2 * part], packed[2 * part : 2 * part + half]
    return jnp.concatenate(
        [
            packed[: 2 * part],
            third,
            pltpu.roll(third, 2 * part, 1),
            pltpu.roll(second, 3 * part, 1),
        ],
        axis=0,
    )


def gram_kernel(
    full, place_ref, env_at, vec_at, wave_ref, env_ref, vec_ref, out_ref, env_out, vec_out, wide, sems
):
    rows, group, size = wave_ref.shape
    places = env_out.shape[0]
    folded = 5 * size // 8
    step = pl.program_id(0)

    def moves():
        for i in range(places):
            yield pltpu.make_async_copy(vec_ref.at[vec_at[i]], vec_out.at[i], sems.at[0, i])
            yield pltpu.make_async_copy(env_ref.at[env_at[i]], env_out.at[i], sems.at[1, i])

    @pl.when(step == 0)
    def _():
        for move in moves():
            move.start()
        if not full:
            out_ref[...] = jnp.zeros_like(out_ref)

    wide[...] = wave_ref[...].astype(jnp.float32).reshape(wide.shape)
    for s in range(group):
        x = wide[pl.ds(s, rows, stride=group), :].astype(jnp.bfloat16)
        gram = lax.dot_general(x, x, (((0,), (0,)), ((), ())), preferred_element_type=jnp.float32)
        out_ref[place_ref[step * group + s]] = fold(gram)

    @pl.when(step == pl.num_programs(0) - 1)
    def _():
        for move in moves():
            move.wait()


def grams_and_moves(wave, env, vectors, place, env_at, vec_at):
    rows, sectors, size = wave.shape
    group = 16
    places = env_at.shape[0]
    folded = 5 * size // 8
    return pl.pallas_call(
        functools.partial(gram_kernel, places * places == sectors),
        grid_spec=pltpu.PrefetchScalarGridSpec(
            num_scalar_prefetch=3,
            grid=(sectors // group,),
            in_specs=[
                pl.BlockSpec((rows, group, size), lambda i, *_: (0, i, 0)),
                pl.BlockSpec(memory_space=pl.ANY),
                pl.BlockSpec(memory_space=pl.ANY),
            ],
            out_specs=[
                pl.BlockSpec((places * places, folded, size), lambda i, *_: (0, 0, 0)),
                pl.BlockSpec(memory_space=pl.ANY),
                pl.BlockSpec(memory_space=pl.ANY),
            ],
            scratch_shapes=[
                pltpu.VMEM((rows * group, size), jnp.float32),
                pltpu.SemaphoreType.DMA((2, places)),
            ],
        ),
        out_shape=[
            jax.ShapeDtypeStruct((places * places, folded, size), jnp.float32),
            jax.ShapeDtypeStruct((places,) + env.shape[1:], env.dtype),
            jax.ShapeDtypeStruct((places,) + vectors.shape[1:], vectors.dtype),
        ],
        compiler_params=pltpu.CompilerParams(vmem_limit_bytes=VMEM_BYTES),
        cost_estimate=pl.CostEstimate(
            flops=2 * rows * sectors * size * size,
            bytes_accessed=2 * rows * sectors * size + 4 * sectors * folded * size,
            transcendentals=0,
        ),
    )(place, env_at, vec_at, wave, env, vectors)


def greet(to_signal, count):
    barrier = pltpu.get_barrier_semaphore()
    for device in to_signal:
        pl.semaphore_signal(barrier, inc=1, device_id=device, device_id_type=MESH)
    pl.semaphore_wait(barrier, count)


def halving_kernel(devices, in_ref, out_ref, total, landed, send_sem, recv_sem):
    me = lax.axis_index("sec")
    segment = lax.axis_index("seg")
    rows = in_ref.shape[1]
    bits = [1 << i for i in range(devices.bit_length() - 1)]

    def partner(bit):
        return (segment, me + bit * (1 - 2 * ((me // bit) % 2)))

    greet([partner(bit) for bit in bits], len(bits))
    orders = [bits, bits[:1] + bits[:0:-1]]
    half = rows // 2
    state = [dict(left=list(range(devices)), used=0) for _ in orders]
    copies = []
    for step in range(len(bits) + 1):
        for h, order in enumerate(orders):
            at = pl.ds(h * half, half)
            now = state[h]
            if step:
                for r, copy, n in now["pending"]:
                    copy.wait_recv()
                    mine = in_ref[r, at, :] if step == 1 else total[r, at, :]
                    if step == len(bits):
                        out_ref[at, :] = mine + landed[h, n]
                    else:
                        total[r, at, :] = mine + landed[h, n]
            if step == len(bits):
                continue
            bit = order[step]
            source = in_ref if step == 0 else total
            keep = [r for r in now["left"] if not r & bit]
            now["pending"] = []
            for i, r in enumerate(keep):
                n = now["used"] + i
                copy = pltpu.make_async_remote_copy(
                    src_ref=source.at[r + bit, at],
                    dst_ref=landed.at[h, n],
                    send_sem=send_sem.at[h, n],
                    recv_sem=recv_sem.at[h, n],
                    device_id=partner(bit),
                    device_id_type=MESH,
                )
                copy.start()
                copies.append(copy)
                now["pending"].append((r, copy, n))
            now["left"] = keep
            now["used"] += len(keep)
    for copy in copies:
        copy.wait_send()


def reduce_scattered(parts):
    devices, rows, size = parts.shape
    return pl.pallas_call(
        functools.partial(halving_kernel, devices),
        in_specs=[pl.BlockSpec(memory_space=pltpu.VMEM)],
        out_specs=pl.BlockSpec(memory_space=pltpu.VMEM),
        out_shape=jax.ShapeDtypeStruct((rows, size), jnp.float32),
        scratch_shapes=[
            pltpu.VMEM(parts.shape, jnp.float32),
            pltpu.VMEM((2, devices - 1, rows // 2, size), jnp.float32),
            pltpu.SemaphoreType.DMA((2, devices - 1)),
            pltpu.SemaphoreType.DMA((2, devices - 1)),
        ],
        compiler_params=pltpu.CompilerParams(
            collective_id=0, has_side_effects=True, vmem_limit_bytes=VMEM_BYTES
        ),
        cost_estimate=pl.CostEstimate(
            flops=devices * rows * size, bytes_accessed=4 * devices * rows * size, transcendentals=0
        ),
    )(parts)


def spread_kernel(
    devices, segments, vec_ref, low_ref, vec_out, low_out, vec_send, vec_recv, low_sems, own_sem
):
    me = lax.axis_index("sec")
    segment = lax.axis_index("seg")
    below = lax.rem(segment + segments - 1, segments)
    above = lax.rem(segment + 1, segments)
    peers = [(segment, lax.rem(me + k, devices)) for k in range(1, devices)]
    greet(peers + [(above, me)], devices)
    low = pltpu.make_async_remote_copy(
        src_ref=low_ref,
        dst_ref=low_out,
        send_sem=low_sems.at[0],
        recv_sem=low_sems.at[1],
        device_id=(below, me),
        device_id_type=MESH,
    )
    low.start()
    copies = []
    for k in range(1, devices):
        copy = pltpu.make_async_remote_copy(
            src_ref=vec_ref.at[k],
            dst_ref=vec_out.at[devices - k],
            send_sem=vec_send.at[k],
            recv_sem=vec_recv.at[devices - k],
            device_id=peers[k - 1],
            device_id_type=MESH,
        )
        copy.start()
        copies.append(copy)
    own = pltpu.make_async_copy(vec_ref.at[0], vec_out.at[0], own_sem)
    own.start()
    own.wait()
    for copy in copies:
        copy.wait()
    low.wait()


def spread_out(vectors, low):
    devices = vectors.shape[0]
    return pl.pallas_call(
        functools.partial(spread_kernel, devices, lax.axis_size("seg")),
        in_specs=[pl.BlockSpec(memory_space=pl.ANY)] * 2,
        out_specs=[pl.BlockSpec(memory_space=pl.ANY)] * 2,
        out_shape=[
            jax.ShapeDtypeStruct(vectors.shape, vectors.dtype),
            jax.ShapeDtypeStruct(low.shape, low.dtype),
        ],
        scratch_shapes=[
            pltpu.SemaphoreType.DMA((devices,)),
            pltpu.SemaphoreType.DMA((devices,)),
            pltpu.SemaphoreType.DMA((2,)),
            pltpu.SemaphoreType.DMA,
        ],
        compiler_params=pltpu.CompilerParams(
            collective_id=1, has_side_effects=True, vmem_limit_bytes=VMEM_BYTES
        ),
        cost_estimate=pl.CostEstimate(
            flops=0, bytes_accessed=4 * vectors.size + 8 * low.size, transcendentals=0
        ),
    )(vectors, low)


def factor_kernel(total_rows, kept_ref, gram_ref, out_ref, c):
    width, size, _ = out_ref.shape
    folded = gram_ref.shape[0] // width
    row_at = lax.broadcasted_iota(jnp.int32, (size, size), 0)
    col_at = lax.broadcasted_iota(jnp.int32, (size, size), 1)
    ridge = jnp.where(row_at == col_at, 0.1, 0.0).astype(jnp.float32)
    for s in range(width):
        c[pl.ds(s, size, stride=width), :] = (
            unfold(gram_ref[s * folded : (s + 1) * folded, :], size) * (1.0 / total_rows) + ridge
        )
    lane = lax.broadcasted_iota(jnp.int32, (width, size), 1)

    def spread(row, at):
        return jnp.broadcast_to(row[:, at : at + 1], (width, size))

    for p in range(0, size, PANEL):
        rows = [c[(p + k) * width : (p + k + 1) * width, :] for k in range(PANEL)]
        corner = {
            (k, l): spread(rows[k], p + l) for k in range(PANEL) for l in range(k, PANEL)
        }
        inside = (lane >= p) & (lane < p + PANEL)
        rows = [
            jnp.where(inside, jnp.where(lane == p + k, 1.0, 0.0), rows[k]) for k in range(PANEL)
        ]
        for k in range(PANEL):
            pivot = corner[k, k]
            r = lax.rsqrt(pivot)
            r = r * (1.5 - 0.5 * pivot * r * r)
            rows[k] = rows[k] * r
            m = {l: corner[k, l] * r for l in range(k + 1, PANEL)}
            for l in range(k + 1, PANEL):
                for j in range(l, PANEL):
                    corner[l, j] = corner[l, j] - m[l] * m[j]
                rows[l] = rows[l] - m[l] * rows[k]
        for k in range(PANEL):
            c[(p + k) * width : (p + k + 1) * width, :] = rows[k]
        for i in range(p + PANEL, size):
            row = jnp.where(inside, 0.0, c[i * width : (i + 1) * width, :])
            first = spread(rows[0], i) * rows[0]
            second = spread(rows[1], i) * rows[1]
            for k in range(2, PANEL, 2):
                first += spread(rows[k], i) * rows[k]
                second += spread(rows[k + 1], i) * rows[k + 1]
            c[i * width : (i + 1) * width, :] = row - (first + second)
    for s in range(width):
        full = c[pl.ds(s, size, stride=width), :]
        keep = (col_at <= row_at) & (row_at < kept_ref[s])
        out_ref[s] = jnp.where(keep, full, 0.0)


def low_inverses(gram_sum, kept_here, total_rows):
    width = kept_here.shape[0]
    size = gram_sum.shape[1]
    return pl.pallas_call(
        functools.partial(factor_kernel, total_rows),
        in_specs=[
            pl.BlockSpec(memory_space=pltpu.SMEM),
            pl.BlockSpec(memory_space=pltpu.VMEM),
        ],
        out_specs=pl.BlockSpec(memory_space=pltpu.VMEM),
        out_shape=jax.ShapeDtypeStruct((width, size, size), jnp.float32),
        scratch_shapes=[pltpu.VMEM((size * width, size), jnp.float32)],
        compiler_params=pltpu.CompilerParams(vmem_limit_bytes=VMEM_BYTES),
        cost_estimate=pl.CostEstimate(
            flops=16 * size**3 * width, bytes_accessed=6 * size * size * width, transcendentals=0
        ),
    )(kept_here, gram_sum)


def split(value):
    high = value.astype(jnp.bfloat16)
    return high, (value - high.astype(jnp.float32)).astype(jnp.bfloat16)


def matvec_kernel(
    devices, segments, low_ref, env_ref, vec_ref, weight_ref, out_ref, y, t, result, send_sem, recv_sem
):
    me = lax.axis_index("sec")
    segment = lax.axis_index("seg")
    below = lax.rem(segment + segments - 1, segments)
    above = lax.rem(segment + 1, segments)
    step = pl.program_id(0)
    channels, columns = weight_ref.shape
    size = low_ref.shape[1]

    def send(k):
        return pltpu.make_async_remote_copy(
            src_ref=result.at[k],
            dst_ref=out_ref.at[lax.rem(devices - k, devices)],
            send_sem=send_sem.at[k],
            recv_sem=recv_sem.at[lax.rem(devices - k, devices)],
            device_id=(above, lax.rem(me + k, devices)),
            device_id_type=MESH,
        )

    @pl.when(step == 0)
    def _():
        greet([(below, lax.rem(me + k, devices)) for k in range(devices)], devices)

    high, low = split(low_ref[0])

    @pl.when(segment != segments - 1)
    def _():
        env = env_ref[0]
        y[...] = lax.dot_general(
            jnp.concatenate([env, env], axis=1),
            jnp.concatenate([high, low], axis=1),
            (((1,), (1,)), ((), ())),
            preferred_element_type=jnp.float32,
        )

    @pl.when(segment == segments - 1)
    def _():
        y[...] = jnp.zeros_like(y)
        y[pl.ds(0, size, stride=channels), :] = low_ref[0].T

    left = jnp.concatenate([high, low, high], axis=1)
    for w in range(0, channels, 2):
        pairs = [split(y[pl.ds(w + z, size, stride=channels), :]) for z in range(2)]
        y_high = jnp.concatenate([pair[0] for pair in pairs], axis=1)
        y_low = jnp.concatenate([pair[1] for pair in pairs], axis=1)
        t[:, w * size : (w + 2) * size] = jnp.dot(
            left,
            jnp.concatenate([y_high, y_high, y_low], axis=0),
            preferred_element_type=jnp.float32,
        ).astype(jnp.bfloat16)
    chunk = 256
    for at in range(0, columns, chunk):
        v = vec_ref[0, :, at : at + chunk].astype(jnp.float32)
        total = None
        for w in range(0, channels, 2):
            scaled = jnp.concatenate(
                [
                    (v * weight_ref[w + z : w + z + 1, at : at + chunk]).astype(jnp.bfloat16)
                    for z in range(2)
                ],
                axis=0,
            )
            term = jnp.dot(
                t[:, w * size : (w + 2) * size], scaled, preferred_element_type=jnp.float32
            )
            total = term if total is None else total + term
        result[step, :, at : at + chunk] = total.astype(jnp.bfloat16)
    send(step).start()

    @pl.when(step == devices - 1)
    def _():
        for k in range(devices):
            send(k).wait()


def matvecs(low, env, vectors, weights):
    devices, size, columns = vectors.shape
    channels = weights.shape[0]
    return pl.pallas_call(
        functools.partial(matvec_kernel, devices, lax.axis_size("seg")),
        grid=(devices,),
        in_specs=[
            pl.BlockSpec((1, size, size), lambda i: (i, 0, 0)),
            pl.BlockSpec((1, size * channels, size), lambda i: (i, 0, 0)),
            pl.BlockSpec((1, size, columns), lambda i: (i, 0, 0)),
            pl.BlockSpec((channels, columns), lambda i: (0, 0)),
        ],
        out_specs=pl.BlockSpec(memory_space=pl.ANY),
        scratch_shapes=[
            pltpu.VMEM((size * channels, size), jnp.float32),
            pltpu.VMEM((size, size * channels), jnp.bfloat16),
            pltpu.VMEM(vectors.shape, jnp.bfloat16),
            pltpu.SemaphoreType.DMA((devices,)),
            pltpu.SemaphoreType.DMA((devices,)),
        ],
        out_shape=jax.ShapeDtypeStruct(vectors.shape, jnp.bfloat16),
        compiler_params=pltpu.CompilerParams(
            collective_id=2, has_side_effects=True, vmem_limit_bytes=VMEM_BYTES
        ),
        cost_estimate=pl.CostEstimate(
            flops=2 * devices * size * size * channels * (2 * size + columns),
            bytes_accessed=2 * devices * size * (channels * size + 2 * columns),
            transcendentals=0,
        ),
    )(low, env, vectors, weights)


def take_kernel(index_ref, in_ref, out_ref, sems):
    moves = [
        pltpu.make_async_copy(in_ref.at[index_ref[i]], out_ref.at[i], sems.at[i])
        for i in range(out_ref.shape[0])
    ]
    for move in moves:
        move.start()
    for move in moves:
        move.wait()


def take_blocks(values, index):
    count = index.shape[0]
    return pl.pallas_call(
        take_kernel,
        in_specs=[
            pl.BlockSpec(memory_space=pltpu.SMEM),
            pl.BlockSpec(memory_space=pl.ANY),
        ],
        out_specs=pl.BlockSpec(memory_space=pl.ANY),
        scratch_shapes=[pltpu.SemaphoreType.DMA((count,))],
        out_shape=jax.ShapeDtypeStruct((count,) + values.shape[1:], values.dtype),
        compiler_params=pltpu.CompilerParams(vmem_limit_bytes=VMEM_BYTES),
        cost_estimate=pl.CostEstimate(
            flops=0, bytes_accessed=4 * count * values[0].size, transcendentals=0
        ),
    )(index, values)


def on_device(
    wave_block, left_envs, next_vectors, site_weights, kept_counts, slots_before, slots_after
):
    devices = lax.axis_size("sec")
    myself = lax.axis_index("sec")
    _, width, size, channels, _ = left_envs.shape
    total_rows = wave_block.shape[1] * devices
    inv_before = inverse_of(slots_before)
    inv_after = inverse_of(slots_after)
    mine_before = lax.dynamic_slice_in_dim(slots_before, myself * width, width)
    mine_after = lax.dynamic_slice_in_dim(slots_after, myself * width, width)
    before_owner = pick(inv_before, mine_after) // width
    after_owner = pick(inv_after, mine_before) // width
    order = lax.rem(myself + jnp.arange(devices, dtype=jnp.int32), devices)
    env_at = place_for(after_owner, order)
    vec_at = place_for(before_owner, order)
    holder, goal = inv_before // width, inv_after // width
    place = (holder ^ myself) * devices + (goal - holder + devices) % devices

    weights = ring(site_weights[0], "seg", -1)
    env = left_envs[0].reshape(width, size * channels, size)
    parts, env, packed = grams_and_moves(
        wave_block[0], env, next_vectors[0], place, env_at, vec_at
    )
    packed = ring(packed, "seg", -1)
    gram_sum = reduce_scattered(parts.reshape(devices, -1, size))
    kept_here = pick(kept_counts, pick(mine_before, env_at))
    low = low_inverses(gram_sum, kept_here, total_rows)
    vectors, low = spread_out(packed, low)
    returned = matvecs(low, env, vectors, weights)
    return take_blocks(returned, (before_owner - myself + devices) % devices)[None]


def solution(mesh):
    placed = (
        P("seg", "sec", None, None),
        P("seg", "sec", None, None, None),
        P("seg", "sec", None, None),
        P("seg", None, None),
        P(),
        P(),
        P(),
    )
    return jax.shard_map(
        on_device,
        mesh=mesh,
        in_specs=placed,
        out_specs=P("seg", "sec", None, None),
        check_vma=False,
    )
```

time: 230 us -> 333 us (1.45)
  Pallas kernels: 51.4 us -> 313 us
  blocking collectives: 73 us -> 0 us
  waiting for transfers between devices: 77.6 us -> 8.03 us
  between operations: 13.5 us -> 0.24 us
    pallas_call x4 -> x5, Pallas kernels: 34.9 us -> 297 us  [the longest x1 195 us: grams_and_moves(): pl.pallas_call(functools.partial(gram_kernel, places * places == sectors)...]
    all_to_all x2 -> x0, blocking collectives: 73 us -> none  [the longest x1 43.3 us: on_device(): lax.all_to_all(packed, 'sec', split_axis=0, concat_axis=0, tiled=True)]
    ppermute x4 -> x2, waiting for transfers between devices: 66.7 us -> 8.03 us  [ring(): lax.ppermute(value, axis, [(i, (i + step) % count) for i in range(count)])]
    reduce_scatter x1 -> x0, waiting for transfers between devices: 10.9 us -> none  [on_device(): lax.psum_scatter(grams(wave_block[0], inv_before), 'sec', scatter_dimensi...]
    ppermute x4 -> x2, starting transfers between devices: 8.57 us -> 5.56 us  [ring(): lax.ppermute(value, axis, [(i, (i + step) % count) for i in range(count)])]
  transfers between devices with their start and end apart: 5 -> 2, of which waited for: 3 -> 1; matrix products, arithmetic and copies ran while one was open for 1% -> 0% of each run, Pallas kernels for 10% -> 18%
where the time goes in v1:
time: 333 us
  Pallas kernels  313 us (94%)
  waiting for transfers between devices  8.03 us (2%)
  starting transfers between devices  5.56 us (2%)
  local copies, waits for them, and re-layouts  4.79 us (1%)
    pallas_call x1, Pallas kernels, grams_and_moves(): pl.pallas_call(functools.partial(gram_kernel, places * places == sectors)...  195 us
    pallas_call x1, Pallas kernels, matvecs(): pl.pallas_call(functools.partial(matvec_kernel, devices, lax.axis_size('s...  54.7 us
    pallas_call x1, Pallas kernels, spread_out(): pl.pallas_call(functools.partial(spread_kernel, devices, lax.axis_size('s...  25.6 us
    pallas_call x1, Pallas kernels, reduce_scattered(): pl.pallas_call(functools.partial(halving_kernel, devices), in_specs=[pl.B...  19.1 us
    pallas_call x1, Pallas kernels, low_inverses(): pl.pallas_call(functools.partial(factor_kernel, total_rows), in_specs=[pl...  16.2 us
    ppermute x2, waiting for transfers between devices, ring(): lax.ppermute(value, axis, [(i, (i + step) % count) for i in range(count)])  8.03 us
  transfers between devices with their start and end apart: 2, of which 1 were waited for; matrix products, arithmetic and copies ran while one was open for 0% of the time, Pallas kernels for 18%

profile of v1, /device:TPU:0, one launch (start us, length us, event | category | flops | bytes accessed | tf_op | source)
XLA Modules:
  0.0 333.2 jit_solution(9834829116563612661)
XLA Ops:
  0.0 0.7 dynamic_slice.7
  0.7 0.7 dynamic_slice.6
  1.5 0.8 select_reduce_fusion
  2.2 0.2 select_reduce_fusion.7
  2.4 0.2 select_reduce_fusion.6
  2.7 0.2 select_reduce_fusion.4
  2.8 0.0 copy-start.1
  2.8 1.6 copy-done.1
  4.4 0.0 copy-start.2
  4.4 195.2 %shard_map.73 = (f32[64,80,128]{2,1,0:T(8,128)}, bf16[8,3072,128]{2,1,0:T(8,128)(2,1)}, bf16[8,128,1024]{2,1,0:T(8,128)(2,1)S(1)}) custom-call(s32[64]{0:T(128)S(1)} %fusion.place_ref, s32[8]{0:T(128)S(1)} %get-tuple-element.16.env_at, s32[8]{0:T(128)S(1)} %get-tuple-element.15.vec_at, bf16[256,64,128]{2,1,0:T(8,128)(2,1)} %bitcast.9, ...), custom_call_target="tpu_custom_call" | custom-call | flops 536870912 | bytes 6815744 | tf_op jit(solution)/shard_map/pallas_call | solution.py:102
  199.7 0.0 copy-start.3
  199.7 5.1 %collective-permute-start = (bf16[8,128,1024]{2,1,0:T(8,128)(2,1)S(1)}, bf16[8,128,1024]{2,1,0:T(8,128)(2,1)S(1)}, u32[]{:S(2)}, u32[]{:S(2)}) collective-permute-start(bf16[8,128,1024]{2,1,0:T(8,128)(2,1)S(1)} %get-tuple-element.10), channel_id=1, source_target_pairs={{0,24},{8,0},{16,8},{24,16},{1,25},{9,1},{17,9},{25,17},{2,26},{10... | collective-permute-start | bytes 6291464 | tf_op jit(solution)/shard_map/ppermute | solution.py:17
  204.8 0.0 copy-done.2
  204.8 0.4 collective-permute-start.1
  205.2 0.0 copy-start
  205.2 1.7 copy-done
  207.0 19.1 %shard_map.74.gram_ref = f32[640,128]{1,0:T(8,128)S(1)} custom-call(f32[8,640,128]{2,1,0:T(8,128)S(1)} %bitcast.6), custom_call_target="tpu_custom_call" | custom-call | flops 655360 | bytes 2621440 | tf_op jit(solution)/shard_map/pallas_call | solution.py:196
  226.1 0.2 select_reduce_fusion.3
  226.2 0.0 copy-done.3
  226.2 0.2 select_reduce_fusion.2.kept_ref
  226.4 16.2 %shard_map.75.low_ref = f32[8,128,128]{2,1,0:T(8,128)S(1)} custom-call(s32[8]{0:T(128)S(1)} %select_reduce_fusion.2.kept_ref, f32[640,128]{1,0:T(8,128)S(1)} %shard_map.74.gram_ref), custom_call_target="tpu_custom_call" | custom-call | flops 268435456 | bytes 786432 | tf_op jit(solution)/shard_map/pallas_call | solution.py:332
  242.7 8.0 %collective-permute-done.vec_ref = bf16[8,128,1024]{2,1,0:T(8,128)(2,1)S(1)} collective-permute-done((bf16[8,128,1024]{2,1,0:T(8,128)(2,1)S(1)}, bf16[8,128,1024]{2,1,0:T(8,128)(2,1)S(1)}, u32[]{:S(2)}, u32[]{:S(2)}) %collective-permute-start) | collective-permute-done | bytes 2097184 | tf_op jit(solution)/shard_map/ppermute | solution.py:17
  250.7 25.6 %shard_map.76 = (bf16[8,128,1024]{2,1,0:T(8,128)(2,1)S(1)}, f32[8,128,128]{2,1,0:T(8,128)S(1)}) custom-call(bf16[8,128,1024]{2,1,0:T(8,128)(2,1)S(1)} %collective-permute-done.vec_ref, f32[8,128,128]{2,1,0:T(8,128)S(1)} %shard_map.75.low_ref), custom_call_target="tpu_custom_call" | custom-call | bytes 5242880 | tf_op jit(solution)/shard_map/pallas_call | solution.py:256
  276.4 0.0 collective-permute-done.1.weight_ref
  276.4 54.7 %shard_map.77.in_ref = bf16[8,128,1024]{2,1,0:T(8,128)(2,1)S(1)} custom-call(f32[8,128,128]{2,1,0:T(8,128)S(1)} %get-tuple-element.12.low_ref, bf16[8,3072,128]{2,1,0:T(8,128)(2,1)} %get-tuple-element.13.env_ref, bf16[8,128,1024]{2,1,0:T(8,128)(2,1)S(1)} %get-tuple-element.14.vec_ref, f32[24,1024]{1,0:T(8,128)S(1)} %collective-permute-done.1.weight_ref), custom_call_target="tpu_custom_call" | custom-call | flops 8053063680 | bytes 10485760 | tf_op jit(solution)/shard_map/pallas_call | solution.py:433
  331.1 1.9 shard_map.78
  (4 shorter events, 0.1 us)
Async XLA Ops:
  2.8 1.6 copy-start.1
  4.4 200.3 %copy-start.2 = (f32[1,24,1024]{2,1,0:T(8,128)S(1)}, f32[1,24,1024]{2,1,0:T(8,128)}, u32[]{:S(2)}) copy-start(f32[1,24,1024]{2,1,0:T(8,128)} %param.10) | copy-start | bytes 294916
  199.7 26.6 %copy-start.3 = (s32[64]{0:T(128)S(1)}, s32[64]{0:T(128)}, u32[]{:S(2)}) copy-start(s32[64]{0:T(128)} %param.11) | copy-start | bytes 772
  199.7 51.0 %collective-permute-start = (bf16[8,128,1024]{2,1,0:T(8,128)(2,1)S(1)}, bf16[8,128,1024]{2,1,0:T(8,128)(2,1)S(1)}, u32[]{:S(2)}, u32[]{:S(2)}) collective-permute-start(bf16[8,128,1024]{2,1,0:T(8,128)(2,1)S(1)} %get-tuple-element.10), channel_id=1, source_target_pairs={{0,24},{8,0},{16,8},{24,16},{1,25},{9,1},{17,9},{25,17},{2,26},{10... | collective-permute-start | bytes 6291464 | tf_op jit(solution)/shard_map/ppermute | solution.py:17
  204.8 71.6 %collective-permute-start.1 = (f32[24,1024]{1,0:T(8,128)S(1)}, f32[24,1024]{1,0:T(8,128)S(1)}, u32[]{:S(2)}, u32[]{:S(2)}) collective-permute-start(f32[24,1024]{1,0:T(8,128)S(1)} %bitcast.10), channel_id=1, source_target_pairs={{0,24},{8,0},{16,8},{24,16},{1,25},{9,1},{17,9},{25,17},{2,26},{10... | collective-permute-start | bytes 294920 | tf_op jit(solution)/shard_map/ppermute | solution.py:17
  205.2 1.7 copy-start

commit v2 on v1

--- a/solution.py
+++ b/solution.py
@@ -63,22 +63,23 @@
 
 
 def gram_kernel(
-    full, place_ref, env_at, vec_at, wave_ref, env_ref, vec_ref, out_ref, env_out, vec_out, wide, sems
+    full, place_ref, env_at, wave_ref, env_ref, out_ref, env_out, wide, staged, sems
 ):
     rows, group, size = wave_ref.shape
     places = env_out.shape[0]
-    folded = 5 * size // 8
     step = pl.program_id(0)
-
-    def moves():
-        for i in range(places):
-            yield pltpu.make_async_copy(vec_ref.at[vec_at[i]], vec_out.at[i], sems.at[0, i])
-            yield pltpu.make_async_copy(env_ref.at[env_at[i]], env_out.at[i], sems.at[1, i])
+    loads = [
+        pltpu.make_async_copy(env_ref.at[env_at[i]], staged.at[i], sems.at[0, i])
+        for i in range(places)
+    ]
+    stores = [
+        pltpu.make_async_copy(staged.at[i], env_out.at[i], sems.at[1, i]) for i in range(places)
+    ]
 
     @pl.when(step == 0)
     def _():
-        for move in moves():
-            move.start()
+        for load in loads:
+            load.start()
         if not full:
             out_ref[...] = jnp.zeros_like(out_ref)
 
@@ -88,13 +89,19 @@
         gram = lax.dot_general(x, x, (((0,), (0,)), ((), ())), preferred_element_type=jnp.float32)
         out_ref[place_ref[step * group + s]] = fold(gram)
 
+    @pl.when(step == pl.num_programs(0) // 2)
+    def _():
+        for load, store in zip(loads, stores):
+            load.wait()
+            store.start()
+
     @pl.when(step == pl.num_programs(0) - 1)
     def _():
-        for move in moves():
-            move.wait()
-
-
-def grams_and_moves(wave, env, vectors, place, env_at, vec_at):
+        for store in stores:
+            store.wait()
+
+
+def grams_and_moves(wave, env, place, env_at):
     rows, sectors, size = wave.shape
     group = 16
     places = env_at.shape[0]
@@ -102,27 +109,25 @@
     return pl.pallas_call(
         functools.partial(gram_kernel, places * places == sectors),
         grid_spec=pltpu.PrefetchScalarGridSpec(
-            num_scalar_prefetch=3,
+            num_scalar_prefetch=2,
             grid=(sectors // group,),
             in_specs=[
                 pl.BlockSpec((rows, group, size), lambda i, *_: (0, i, 0)),
-                pl.BlockSpec(memory_space=pl.ANY),
                 pl.BlockSpec(memory_space=pl.ANY),
             ],
             out_specs=[
                 pl.BlockSpec((places * places, folded, size), lambda i, *_: (0, 0, 0)),
                 pl.BlockSpec(memory_space=pl.ANY),
-                pl.BlockSpec(memory_space=pl.ANY),
             ],
             scratch_shapes=[
                 pltpu.VMEM((rows * group, size), jnp.float32),
+                pltpu.VMEM((places,) + env.shape[1:], env.dtype),
                 pltpu.SemaphoreType.DMA((2, places)),
             ],
         ),
         out_shape=[
             jax.ShapeDtypeStruct((places * places, folded, size), jnp.float32),
             jax.ShapeDtypeStruct((places,) + env.shape[1:], env.dtype),
-            jax.ShapeDtypeStruct((places,) + vectors.shape[1:], vectors.dtype),
         ],
         compiler_params=pltpu.CompilerParams(vmem_limit_bytes=VMEM_BYTES),
         cost_estimate=pl.CostEstimate(
@@ -130,7 +135,7 @@
             bytes_accessed=2 * rows * sectors * size + 4 * sectors * folded * size,
             transcendentals=0,
         ),
-    )(place, env_at, vec_at, wave, env, vectors)
+    )(place, env_at, wave, env)
 
 
 def greet(to_signal, count):
@@ -213,69 +218,6 @@
     )(parts)
 
 
-def spread_kernel(
-    devices, segments, vec_ref, low_ref, vec_out, low_out, vec_send, vec_recv, low_sems, own_sem
-):
-    me = lax.axis_index("sec")
-    segment = lax.axis_index("seg")
-    below = lax.rem(segment + segments - 1, segments)
-    above = lax.rem(segment + 1, segments)
-    peers = [(segment, lax.rem(me + k, devices)) for k in range(1, devices)]
-    greet(peers + [(above, me)], devices)
-    low = pltpu.make_async_remote_copy(
-        src_ref=low_ref,
-        dst_ref=low_out,
-        send_sem=low_sems.at[0],
-        recv_sem=low_sems.at[1],
-        device_id=(below, me),
-        device_id_type=MESH,
-    )
-    low.start()
-    copies = []
-    for k in range(1, devices):
-        copy = pltpu.make_async_remote_copy(
-            src_ref=vec_ref.at[k],
-            dst_ref=vec_out.at[devices - k],
-            send_sem=vec_send.at[k],
-            recv_sem=vec_recv.at[devices - k],
-            device_id=peers[k - 1],
-            device_id_type=MESH,
-        )
-        copy.start()
-        copies.append(copy)
-    own = pltpu.make_async_copy(vec_ref.at[0], vec_out.at[0], own_sem)
-    own.start()
-    own.wait()
-    for copy in copies:
-        copy.wait()
-    low.wait()
-
-
-def spread_out(vectors, low):
-    devices = vectors.shape[0]
-    return pl.pallas_call(
-        functools.partial(spread_kernel, devices, lax.axis_size("seg")),
-        in_specs=[pl.BlockSpec(memory_space=pl.ANY)] * 2,
-        out_specs=[pl.BlockSpec(memory_space=pl.ANY)] * 2,
-        out_shape=[
-            jax.ShapeDtypeStruct(vectors.shape, vectors.dtype),
-            jax.ShapeDtypeStruct(low.shape, low.dtype),
-        ],
-        scratch_shapes=[
-            pltpu.SemaphoreType.DMA((devices,)),
-            pltpu.SemaphoreType.DMA((devices,)),
-            pltpu.SemaphoreType.DMA((2,)),
-            pltpu.SemaphoreType.DMA,
-        ],
-        compiler_params=pltpu.CompilerParams(
-            collective_id=1, has_side_effects=True, vmem_limit_bytes=VMEM_BYTES
-        ),
-        cost_estimate=pl.CostEstimate(
-            flops=0, bytes_accessed=4 * vectors.size + 8 * low.size, transcendentals=0
-        ),
-    )(vectors, low)
-
-
 def factor_kernel(total_rows, kept_ref, gram_ref, out_ref, c):
     width, size, _ = out_ref.shape
     folded = gram_ref.shape[0] // width
@@ -340,7 +282,7 @@
         scratch_shapes=[pltpu.VMEM((size * width, size), jnp.float32)],
         compiler_params=pltpu.CompilerParams(vmem_limit_bytes=VMEM_BYTES),
         cost_estimate=pl.CostEstimate(
-            flops=16 * size**3 * width, bytes_accessed=6 * size * size * width, transcendentals=0
+            flops=1100 * size**3 * width, bytes_accessed=6 * size * size * width, transcendentals=0
         ),
     )(kept_here, gram_sum)
 
@@ -351,8 +293,9 @@
 
 
 def matvec_kernel(
-    devices, segments, low_ref, env_ref, vec_ref, weight_ref, out_ref, y, t, result, send_sem, recv_sem
+    devices, segments, low_ref, env_ref, weight_ref, *refs
 ):
+    vec_refs, (out_ref, y, t, vec, result, send_sem, recv_sem) = refs[:devices], refs[devices:]
     me = lax.axis_index("sec")
     segment = lax.axis_index("seg")
     below = lax.rem(segment + segments - 1, segments)
@@ -374,6 +317,12 @@
     @pl.when(step == 0)
     def _():
         greet([(below, lax.rem(me + k, devices)) for k in range(devices)], devices)
+
+    for k in range(devices):
+
+        @pl.when(step == k)
+        def _(k=k):
+            vec[...] = vec_refs[k][...]
 
     high, low = split(low_ref[0])
 
@@ -404,7 +353,7 @@
         ).astype(jnp.bfloat16)
     chunk = 256
     for at in range(0, columns, chunk):
-        v = vec_ref[0, :, at : at + chunk].astype(jnp.float32)
+        v = vec[:, at : at + chunk].astype(jnp.float32)
         total = None
         for w in range(0, channels, 2):
             scaled = jnp.concatenate(
@@ -428,7 +377,8 @@
 
 
 def matvecs(low, env, vectors, weights):
-    devices, size, columns = vectors.shape
+    devices = len(vectors)
+    size, columns = vectors[0].shape
     channels = weights.shape[0]
     return pl.pallas_call(
         functools.partial(matvec_kernel, devices, lax.axis_size("seg")),
@@ -436,27 +386,28 @@
         in_specs=[
             pl.BlockSpec((1, size, size), lambda i: (i, 0, 0)),
             pl.BlockSpec((1, size * channels, size), lambda i: (i, 0, 0)),
-            pl.BlockSpec((1, size, columns), lambda i: (i, 0, 0)),
             pl.BlockSpec((channels, columns), lambda i: (0, 0)),
-        ],
+        ]
+        + [pl.BlockSpec((size, columns), lambda i: (0, 0), pipeline_mode=pl.Buffered(1))] * devices,
         out_specs=pl.BlockSpec(memory_space=pl.ANY),
         scratch_shapes=[
             pltpu.VMEM((size * channels, size), jnp.float32),
             pltpu.VMEM((size, size * channels), jnp.bfloat16),
-            pltpu.VMEM(vectors.shape, jnp.bfloat16),
+            pltpu.VMEM((size, columns), jnp.bfloat16),
+            pltpu.VMEM((devices, size, columns), jnp.bfloat16),
             pltpu.SemaphoreType.DMA((devices,)),
             pltpu.SemaphoreType.DMA((devices,)),
         ],
-        out_shape=jax.ShapeDtypeStruct(vectors.shape, jnp.bfloat16),
+        out_shape=jax.ShapeDtypeStruct((devices, size, columns), jnp.bfloat16),
         compiler_params=pltpu.CompilerParams(
-            collective_id=2, has_side_effects=True, vmem_limit_bytes=VMEM_BYTES
+            collective_id=1, has_side_effects=True, vmem_limit_bytes=VMEM_BYTES
         ),
         cost_estimate=pl.CostEstimate(
             flops=2 * devices * size * size * channels * (2 * size + columns),
             bytes_accessed=2 * devices * size * (channels * size + 2 * columns),
             transcendentals=0,
         ),
-    )(low, env, vectors, weights)
+    )(low, env, weights, *vectors)
 
 
 def take_kernel(index_ref, in_ref, out_ref, sems):
@@ -481,6 +432,47 @@
         out_specs=pl.BlockSpec(memory_space=pl.ANY),
         scratch_shapes=[pltpu.SemaphoreType.DMA((count,))],
         out_shape=jax.ShapeDtypeStruct((count,) + values.shape[1:], values.dtype),
+        compiler_params=pltpu.CompilerParams(vmem_limit_bytes=VMEM_BYTES),
+        cost_estimate=pl.CostEstimate(
+            flops=0, bytes_accessed=4 * count * values[0].size, transcendentals=0
+        ),
+    )(index, values)
+
+
+def part_kernel(index_ref, in_ref, *refs):
+    count = len(refs) - 2
+    outs, staged, sems = refs[:count], refs[count], refs[count + 1]
+    loads = [
+        pltpu.make_async_copy(in_ref.at[index_ref[i]], staged.at[i], sems.at[0, i])
+        for i in range(count)
+    ]
+    stores = [
+        pltpu.make_async_copy(staged.at[i], outs[i], sems.at[1, i]) for i in range(count)
+    ]
+    for load in loads:
+        load.start()
+    for load, store in zip(loads, stores):
+        load.wait()
+        store.start()
+    for store in stores:
+        store.wait()
+
+
+def parted(values, index):
+    count = index.shape[0]
+    block = values.shape[1:]
+    return pl.pallas_call(
+        part_kernel,
+        in_specs=[
+            pl.BlockSpec(memory_space=pltpu.SMEM),
+            pl.BlockSpec(memory_space=pl.ANY),
+        ],
+        out_specs=[pl.BlockSpec(memory_space=pl.ANY)] * count,
+        scratch_shapes=[
+            pltpu.VMEM((count,) + block, values.dtype),
+            pltpu.SemaphoreType.DMA((2, count)),
+        ],
+        out_shape=[jax.ShapeDtypeStruct(block, values.dtype)] * count,
         compiler_params=pltpu.CompilerParams(vmem_limit_bytes=VMEM_BYTES),
         cost_estimate=pl.CostEstimate(
             flops=0, bytes_accessed=4 * count * values[0].size, transcendentals=0
@@ -503,20 +495,36 @@
     after_owner = pick(inv_after, mine_before) // width
     order = lax.rem(myself + jnp.arange(devices, dtype=jnp.int32), devices)
     env_at = place_for(after_owner, order)
-    vec_at = place_for(before_owner, order)
+    back = lax.rem(myself + devices - jnp.arange(devices, dtype=jnp.int32), devices)
+    vec_at = place_for(before_owner, back)
     holder, goal = inv_before // width, inv_after // width
     place = (holder ^ myself) * devices + (goal - holder + devices) % devices
 
-    weights = ring(site_weights[0], "seg", -1)
     env = left_envs[0].reshape(width, size * channels, size)
-    parts, env, packed = grams_and_moves(
-        wave_block[0], env, next_vectors[0], place, env_at, vec_at
+    segments = lax.axis_size("seg")
+    def sent(block, k):
+        pairs = [
+            (g * devices + p, (g - 1) % segments * devices + (p - k) % devices)
+            for g in range(segments)
+            for p in range(devices)
+        ]
+        return lax.ppermute(block, ("seg", "sec"), pairs)
+
+    blocks = parted(next_vectors[0], vec_at)
+    early = 5 * devices // 8
+    first = [sent(blocks[k], k) for k in range(early)]
+    parts, env = grams_and_moves(wave_block[0], env, place, env_at)
+    gram_sum = reduce_scattered(parts.reshape(devices, -1, size))
+    gram_sum, first, blocks, weights = lax.optimization_barrier(
+        (gram_sum, first, blocks, site_weights[0])
     )
-    packed = ring(packed, "seg", -1)
-    gram_sum = reduce_scattered(parts.reshape(devices, -1, size))
+    weights = ring(weights, "seg", -1)
+    second = [sent(blocks[k], k) for k in range(early, devices)]
     kept_here = pick(kept_counts, pick(mine_before, env_at))
     low = low_inverses(gram_sum, kept_here, total_rows)
-    vectors, low = spread_out(packed, low)
+    low, second, weights = lax.optimization_barrier((low, second, weights))
+    low = ring(low, "seg", -1)
+    vectors = first + second
     returned = matvecs(low, env, vectors, weights)
     return take_blocks(returned, (before_owner - myself + devices) % devices)[None]
 

time: 333 us -> 146 us (0.44)
  Pallas kernels: 313 us -> 105 us
  starting transfers between devices: 5.56 us -> 22.5 us
  waiting for transfers between devices: 8.03 us -> 12.8 us
    pallas_call x1, Pallas kernels: 195 us -> 10.3 us  [grams_and_moves(): pl.pallas_call(functools.partial(gram_kernel, places * places == sectors)...]
    pallas_call x1, Pallas kernels: 25.6 us -> 1.01 us  [parted(): pl.pallas_call(part_kernel, in_specs=[pl.BlockSpec(memory_space=pltpu.SME...]
    ppermute x0 -> x8, starting transfers between devices: none -> 17.3 us  [sent(): return lax.ppermute(block, ('seg', 'sec'), pairs)]
    ppermute x2, waiting for transfers between devices: 8.03 us -> 12.8 us  [ring(): lax.ppermute(value, axis, [(i, (i + step) % count) for i in range(count)])]
  transfers between devices with their start and end apart: 2 -> 10, of which waited for: 1 -> 2; matrix products, arithmetic and copies ran while one was open for 0% -> 2% of each run, Pallas kernels for 18% -> 33%
where the time goes in v2:
time: 146 us
  Pallas kernels  105 us (72%)
  starting transfers between devices  22.5 us (15%)
  waiting for transfers between devices  12.8 us (9%)
  local copies, waits for them, and re-layouts  3.06 us (2%)
  other arithmetic  2.65 us (2%)
    pallas_call x1, Pallas kernels, matvecs(): pl.pallas_call(functools.partial(matvec_kernel, devices, lax.axis_size('s...  53.4 us
    pallas_call x1, Pallas kernels, reduce_scattered(): pl.pallas_call(functools.partial(halving_kernel, devices), in_specs=[pl.B...  21.7 us
    ppermute x8, starting transfers between devices, sent(): return lax.ppermute(block, ('seg', 'sec'), pairs)  17.3 us
    pallas_call x1, Pallas kernels, low_inverses(): pl.pallas_call(functools.partial(factor_kernel, total_rows), in_specs=[pl...  16.3 us
    ppermute x2, waiting for transfers between devices, ring(): lax.ppermute(value, axis, [(i, (i + step) % count) for i in range(count)])  12.8 us
    pallas_call x1, Pallas kernels, grams_and_moves(): pl.pallas_call(functools.partial(gram_kernel, places * places == sectors)...  10.3 us
    ppermute x2, starting transfers between devices, ring(): lax.ppermute(value, axis, [(i, (i + step) % count) for i in range(count)])  5.23 us
  transfers between devices with their start and end apart: 10, of which 2 were waited for; matrix products, arithmetic and copies ran while one was open for 2% of the time, Pallas kernels for 33%

profile of v2, /device:TPU:0, one launch (start us, length us, event | category | flops | bytes accessed | tf_op | source)
XLA Modules:
  0.0 145.9 jit_solution(1932107636430757354)
XLA Ops:
  0.0 0.7 select_reduce_fusion.1
  0.7 0.7 dynamic_slice.6
  1.5 0.2 select_reduce_fusion.7
  1.7 0.2 select_reduce_fusion.2.index_ref
  1.9 1.6 %copy-done = bf16[1,8,128,1024]{3,2,1,0:T(8,128)(2,1)S(1)} copy-done((bf16[1,8,128,1024]{3,2,1,0:T(8,128)(2,1)S(1)}, bf16[1,8,128,1024]{3,2,1,0:T(8,128)(2,1)}, u32[]{:S(2)}) %copy-start) | copy-done | bytes 2097176
  3.5 1.0 shard_map.75
  4.5 5.1 %collective-permute-start = (bf16[128,1024]{1,0:T(8,128)(2,1)S(1)}, bf16[128,1024]{1,0:T(8,128)(2,1)S(1)}, u32[]{:S(2)}, u32[]{:S(2)}) collective-permute-start(bf16[128,1024]{1,0:T(8,128)(2,1)S(1)} %get-tuple-element.31), channel_id=1, source_target_pairs={{0,24},{1,25},{2,26},{3,27},{4,28},{5,29},{6,30},{7,31},{8,0},{9,1... | collective-permute-start | bytes 786440 | tf_op jit(solution)/shard_map/ppermute | solution.py:511
  9.6 1.5 %collective-permute-start.1 = (bf16[128,1024]{1,0:T(8,128)(2,1)S(1)}, bf16[128,1024]{1,0:T(8,128)(2,1)S(1)}, u32[]{:S(2)}, u32[]{:S(2)}) collective-permute-start(bf16[128,1024]{1,0:T(8,128)(2,1)S(1)} %get-tuple-element.32), channel_id=1, source_target_pairs={{0,31},{1,24},{2,25},{3,26},{4,27},{5,28},{6,29},{7,30},{8,7},{9,0... | collective-permute-start | bytes 786440 | tf_op jit(solution)/shard_map/ppermute | solution.py:511
  11.1 0.8 collective-permute-start.2
  11.9 0.3 collective-permute-start.3
  12.2 4.6 %collective-permute-start.4 = (bf16[128,1024]{1,0:T(8,128)(2,1)S(1)}, bf16[128,1024]{1,0:T(8,128)(2,1)S(1)}, u32[]{:S(2)}, u32[]{:S(2)}) collective-permute-start(bf16[128,1024]{1,0:T(8,128)(2,1)S(1)} %get-tuple-element.35), channel_id=1, source_target_pairs={{0,28},{1,29},{2,30},{3,31},{4,24},{5,25},{6,26},{7,27},{8,4},{9,5... | collective-permute-start | bytes 786440 | tf_op jit(solution)/shard_map/ppermute | solution.py:511
  16.8 0.7 dynamic_slice.7
  17.5 0.7 select_reduce_fusion
  18.3 0.2 select_reduce_fusion.6
  18.5 0.2 select_reduce_fusion.5.env_at
  18.6 10.3 %shard_map.73 = (f32[64,80,128]{2,1,0:T(8,128)S(1)}, bf16[8,3072,128]{2,1,0:T(8,128)(2,1)}) custom-call(s32[64]{0:T(128)S(1)} %fusion.place_ref, s32[8]{0:T(128)S(1)} %select_reduce_fusion.5.env_at, bf16[256,64,128]{2,1,0:T(8,128)(2,1)} %bitcast.9, bf16[8,3072,128]{2,1,0:T(8,128)(2,1)} %bitcast.8), custom_call_target="tpu_custom_call" | custom-call | flops 536870912 | bytes 6815744 | tf_op jit(solution)/shard_map/pallas_call | solution.py:109
  29.0 0.0 copy-start.2
  29.0 0.0 copy-start.1
  29.0 21.7 %shard_map.74.gram_ref = f32[640,128]{1,0:T(8,128)S(1)} custom-call(f32[8,640,128]{2,1,0:T(8,128)S(1)} %bitcast.6), custom_call_target="tpu_custom_call" | custom-call | flops 655360 | bytes 2621440 | tf_op jit(solution)/shard_map/pallas_call | solution.py:201
  50.7 0.2 select_reduce_fusion.4
  50.9 0.2 select_reduce_fusion.3.kept_ref
  51.1 0.0 collective-permute-done.refs_0_
  51.1 0.0 collective-permute-done.1.refs_1_
  51.1 3.7 %collective-permute-start.5 = (bf16[128,1024]{1,0:T(8,128)(2,1)S(1)}, bf16[128,1024]{1,0:T(8,128)(2,1)S(1)}, u32[]{:S(2)}, u32[]{:S(2)}) collective-permute-start(bf16[128,1024]{1,0:T(8,128)(2,1)S(1)} %get-tuple-element.40), channel_id=1, source_target_pairs={{0,27},{1,28},{2,29},{3,30},{4,31},{5,24},{6,25},{7,26},{8,3},{9,4... | collective-permute-start | bytes 786440 | tf_op jit(solution)/shard_map/ppermute | solution.py:511
  54.9 1.3 collective-permute-start.6
  56.1 0.8 collective-permute-start.8
  57.0 16.3 %shard_map.76 = f32[8,128,128]{2,1,0:T(8,128)S(1)} custom-call(s32[8]{0:T(128)S(1)} %select_reduce_fusion.3.kept_ref, f32[640,128]{1,0:T(8,128)S(1)} %shard_map.74.gram_ref), custom_call_target="tpu_custom_call" | custom-call | flops 18454937600 | bytes 786432 | tf_op jit(solution)/shard_map/pallas_call | solution.py:274
  73.3 0.5 collective-permute-done.8.weight_ref
  73.8 4.4 %collective-permute-start.9 = (f32[8,128,128]{2,1,0:T(8,128)S(1)}, f32[8,128,128]{2,1,0:T(8,128)S(1)}, u32[]{:S(2)}, u32[]{:S(2)}) collective-permute-start(f32[8,128,128]{2,1,0:T(8,128)S(1)} %shard_map.76), channel_id=1, source_target_pairs={{0,24},{8,0},{16,8},{24,16},{1,25},{9,1},{17,9},{25,17},{2,26},{10... | collective-permute-start | bytes 1572872 | tf_op jit(solution)/shard_map/ppermute | solution.py:17
  78.2 12.2 %collective-permute-done.9.low_ref = f32[8,128,128]{2,1,0:T(8,128)S(1)} collective-permute-done((f32[8,128,128]{2,1,0:T(8,128)S(1)}, f32[8,128,128]{2,1,0:T(8,128)S(1)}, u32[]{:S(2)}, u32[]{:S(2)}) %collective-permute-start.9) | collective-permute-done | bytes 524320 | tf_op jit(solution)/shard_map/ppermute | solution.py:17
  90.4 53.4 %shard_map.77.in_ref = bf16[8,128,1024]{2,1,0:T(8,128)(2,1)S(1)} custom-call(f32[8,128,128]{2,1,0:T(8,128)S(1)} %collective-permute-done.9.low_ref, bf16[8,3072,128]{2,1,0:T(8,128)(2,1)} %get-tuple-element.45.env_ref, f32[24,1024]{1,0:T(8,128)S(1)} %collective-permute-done.8.weight_ref, bf16[128,1024]{1,0:T(8,128)(2,1)S(1)} %collective-permute-done.refs_0_, ...), custom_call_target="tpu_custom_call" | custom-call | flops 8053063680 | bytes 10485760 | tf_op jit(solution)/shard_map/pallas_call | solution.py:383
  143.8 1.9 %shard_map.78 = bf16[8,128,1024]{2,1,0:T(8,128)(2,1)} custom-call(s32[8]{0:T(128)S(1)} %get-tuple-element.55.index_ref, bf16[8,128,1024]{2,1,0:T(8,128)(2,1)S(1)} %shard_map.77.in_ref), custom_call_target="tpu_custom_call" | custom-call | bytes 4194304 | tf_op jit(solution)/shard_map/pallas_call | solution.py:426
  (14 shorter events, 0.1 us)
Async XLA Ops:
  1.9 1.6 %copy-start = (bf16[1,8,128,1024]{3,2,1,0:T(8,128)(2,1)S(1)}, bf16[1,8,128,1024]{3,2,1,0:T(8,128)(2,1)}, u32[]{:S(2)}) copy-start(bf16[1,8,128,1024]{3,2,1,0:T(8,128)(2,1)} %param.9) | copy-start | bytes 6291460
  4.5 46.6 %collective-permute-start = (bf16[128,1024]{1,0:T(8,128)(2,1)S(1)}, bf16[128,1024]{1,0:T(8,128)(2,1)S(1)}, u32[]{:S(2)}, u32[]{:S(2)}) collective-permute-start(bf16[128,1024]{1,0:T(8,128)(2,1)S(1)} %get-tuple-element.31), channel_id=1, source_target_pairs={{0,24},{1,25},{2,26},{3,27},{4,28},{5,29},{6,30},{7,31},{8,0},{9,1... | collective-permute-start | bytes 786440 | tf_op jit(solution)/shard_map/ppermute | solution.py:511
  9.6 41.5 %collective-permute-start.1 = (bf16[128,1024]{1,0:T(8,128)(2,1)S(1)}, bf16[128,1024]{1,0:T(8,128)(2,1)S(1)}, u32[]{:S(2)}, u32[]{:S(2)}) collective-permute-start(bf16[128,1024]{1,0:T(8,128)(2,1)S(1)} %get-tuple-element.32), channel_id=1, source_target_pairs={{0,31},{1,24},{2,25},{3,26},{4,27},{5,28},{6,29},{7,30},{8,7},{9,0... | collective-permute-start | bytes 786440 | tf_op jit(solution)/shard_map/ppermute | solution.py:511
  11.1 40.0 %collective-permute-start.2 = (bf16[128,1024]{1,0:T(8,128)(2,1)S(1)}, bf16[128,1024]{1,0:T(8,128)(2,1)S(1)}, u32[]{:S(2)}, u32[]{:S(2)}) collective-permute-start(bf16[128,1024]{1,0:T(8,128)(2,1)S(1)} %get-tuple-element.33), channel_id=1, source_target_pairs={{0,30},{1,31},{2,24},{3,25},{4,26},{5,27},{6,28},{7,29},{8,6},{9,7... | collective-permute-start | bytes 786440 | tf_op jit(solution)/shard_map/ppermute | solution.py:511
  11.9 39.2 %collective-permute-start.3 = (bf16[128,1024]{1,0:T(8,128)(2,1)S(1)}, bf16[128,1024]{1,0:T(8,128)(2,1)S(1)}, u32[]{:S(2)}, u32[]{:S(2)}) collective-permute-start(bf16[128,1024]{1,0:T(8,128)(2,1)S(1)} %get-tuple-element.34), channel_id=1, source_target_pairs={{0,29},{1,30},{2,31},{3,24},{4,25},{5,26},{6,27},{7,28},{8,5},{9,6... | collective-permute-start | bytes 786440 | tf_op jit(solution)/shard_map/ppermute | solution.py:511
  12.2 38.9 %collective-permute-start.4 = (bf16[128,1024]{1,0:T(8,128)(2,1)S(1)}, bf16[128,1024]{1,0:T(8,128)(2,1)S(1)}, u32[]{:S(2)}, u32[]{:S(2)}) collective-permute-start(bf16[128,1024]{1,0:T(8,128)(2,1)S(1)} %get-tuple-element.35), channel_id=1, source_target_pairs={{0,28},{1,29},{2,30},{3,31},{4,24},{5,25},{6,26},{7,27},{8,4},{9,5... | collective-permute-start | bytes 786440 | tf_op jit(solution)/shard_map/ppermute | solution.py:511
  29.0 22.0 %copy-start.2 = (s32[64]{0:T(128)S(1)}, s32[64]{0:T(128)}, u32[]{:S(2)}) copy-start(s32[64]{0:T(128)} %param.11) | copy-start | bytes 772
  29.0 27.2 %copy-start.1 = (f32[1,24,1024]{2,1,0:T(8,128)S(1)}, f32[1,24,1024]{2,1,0:T(8,128)}, u32[]{:S(2)}) copy-start(f32[1,24,1024]{2,1,0:T(8,128)} %param.10) | copy-start | bytes 294916
  51.1 22.7 %collective-permute-start.5 = (bf16[128,1024]{1,0:T(8,128)(2,1)S(1)}, bf16[128,1024]{1,0:T(8,128)(2,1)S(1)}, u32[]{:S(2)}, u32[]{:S(2)}) collective-permute-start(bf16[128,1024]{1,0:T(8,128)(2,1)S(1)} %get-tuple-element.40), channel_id=1, source_target_pairs={{0,27},{1,28},{2,29},{3,30},{4,31},{5,24},{6,25},{7,26},{8,3},{9,4... | collective-permute-start | bytes 786440 | tf_op jit(solution)/shard_map/ppermute | solution.py:511
  54.9 18.9 %collective-permute-start.6 = (bf16[128,1024]{1,0:T(8,128)(2,1)S(1)}, bf16[128,1024]{1,0:T(8,128)(2,1)S(1)}, u32[]{:S(2)}, u32[]{:S(2)}) collective-permute-start(bf16[128,1024]{1,0:T(8,128)(2,1)S(1)} %get-tuple-element.41), channel_id=1, source_target_pairs={{0,26},{1,27},{2,28},{3,29},{4,30},{5,31},{6,24},{7,25},{8,2},{9,3... | collective-permute-start | bytes 786440 | tf_op jit(solution)/shard_map/ppermute | solution.py:511
  56.1 17.7 %collective-permute-start.7 = (bf16[128,1024]{1,0:T(8,128)(2,1)S(1)}, bf16[128,1024]{1,0:T(8,128)(2,1)S(1)}, u32[]{:S(2)}, u32[]{:S(2)}) collective-permute-start(bf16[128,1024]{1,0:T(8,128)(2,1)S(1)} %get-tuple-element.42), channel_id=1, source_target_pairs={{0,25},{1,26},{2,27},{3,28},{4,29},{5,30},{6,31},{7,24},{8,1},{9,2... | collective-permute-start | bytes 786440 | tf_op jit(solution)/shard_map/ppermute | solution.py:511
  56.1 17.7 %collective-permute-start.8 = (f32[24,1024]{1,0:T(8,128)S(1)}, f32[24,1024]{1,0:T(8,128)S(1)}, u32[]{:S(2)}, u32[]{:S(2)}) collective-permute-start(f32[24,1024]{1,0:T(8,128)S(1)} %bitcast.10), channel_id=1, source_target_pairs={{0,24},{8,0},{16,8},{24,16},{1,25},{9,1},{17,9},{25,17},{2,26},{10... | collective-permute-start | bytes 294920 | tf_op jit(solution)/shard_map/ppermute | solution.py:17
  73.8 16.6 %collective-permute-start.9 = (f32[8,128,128]{2,1,0:T(8,128)S(1)}, f32[8,128,128]{2,1,0:T(8,128)S(1)}, u32[]{:S(2)}, u32[]{:S(2)}) collective-permute-start(f32[8,128,128]{2,1,0:T(8,128)S(1)} %shard_map.76), channel_id=1, source_target_pairs={{0,24},{8,0},{16,8},{24,16},{1,25},{9,1},{17,9},{25,17},{2,26},{10... | collective-permute-start | bytes 1572872 | tf_op jit(solution)/shard_map/ppermute | solution.py:17
